TPU v7x, 32 devices: a whole 2x2x4 slice. The times are simulated.
32 devices in a mesh: expert: 16 (over z, y, x), dp: 2 (over core).
Axes of the slice: x: 2, y: 2, z: 4, core: 2. Of those that a mesh axis runs over, the one named last changes fastest.
Arguments:
- grad_out: bfloat16 [1024, 1792], P(('expert', 'dp')), may hold values from -6 to 6
- expert_ids: int32 [1024, 8], P(('expert', 'dp')), may hold values from 0 to 15, all different within a row; in each aligned block of 32 rows (0 to 31, 32 to 63, ...) at most 24 rows name the same one
- router_weights: bfloat16 [1024, 8], P(('expert', 'dp')), may hold values from 0.019897461 to 0.29882812
- saved_hidden: bfloat16 [2, 16, 16, 24, 1280], P('dp', 'expert'), may hold values from -0.29882812 to 0.29882812
- down_weight: bfloat16 [16, 1280, 1792], P('expert'), may hold values from -0.15625 to 0.15625
Outputs:
- grad_hidden: bfloat16 [2, 16, 16, 24, 1280], P('dp', 'expert')
- grad_weight: bfloat16 [16, 1280, 1792], P('expert', 'dp')
- grad_router: float32 [1024, 8], P(('expert', 'dp'))
Inputs may be any that keep to these rules, and one draw needn't show every extreme that they name: `expert_ids`: each row names 8 different experts. Among the rows held by one device (aligned blocks of 32 rows), no expert is named by more than 24 rows.
All inputs are finite; a program needn't handle non-finite values.
Results may differ from a plain program's by a relative error of at most 0.0058.
Values may be sent and summed in bfloat16 or wider, within the bound.
A program may use at most 64 MiB of HBM per device.

v0:
```python
import jax
import jax.numpy as jnp
from jax import lax
from jax.sharding import PartitionSpec as P


def on_device(grad_out, expert_ids, router_weights, saved_hidden, down_weight):
    experts = lax.axis_size("expert")
    groups = lax.axis_size("dp")
    token_count = grad_out.shape[0]
    top_count = expert_ids.shape[1]
    capacity = saved_hidden.shape[3]
    features = grad_out.shape[1]
    hidden_units = saved_hidden.shape[4]
    flat_ids = expert_ids.reshape(-1)
    onehot = (flat_ids[:, None] == jnp.arange(experts, dtype=jnp.int32)[None, :]).astype(jnp.int32)
    slot_rank = jnp.sum((jnp.cumsum(onehot, axis=0) - onehot) * onehot, axis=1)
    slot_index = flat_ids * capacity + slot_rank
    token_rows = jnp.repeat(grad_out, top_count, axis=0)
    outgoing = (
        jnp.zeros((experts * capacity, features), jnp.bfloat16).at[slot_index].set(token_rows)
    )
    outgoing = outgoing.reshape(experts, capacity, features)
    scales_out = (
        jnp.zeros((experts * capacity,), jnp.bfloat16)
        .at[slot_index]
        .set(router_weights.reshape(-1))
    )
    scales_out = scales_out.reshape(experts, capacity)
    arrived, arrived_scales = (
        lax.all_to_all(outgoing, "expert", split_axis=0, concat_axis=0, tiled=True),
        lax.all_to_all(scales_out, "expert", split_axis=0, concat_axis=0, tiled=True),
    )
    slot_rows = arrived.reshape(experts * capacity, features)
    row_scale = arrived_scales.reshape(-1).astype(jnp.float32)
    hidden_rows = saved_hidden.reshape(experts * capacity, hidden_units)
    weight = down_weight[0]
    projected = lax.dot_general(
        slot_rows, weight, (((1,), (1,)), ((), ())), preferred_element_type=jnp.float32
    )
    grad_hidden = (row_scale[:, None] * projected).astype(jnp.bfloat16)
    grad_hidden = grad_hidden.reshape(1, 1, experts, capacity, hidden_units)
    prob_grad = jnp.sum(hidden_rows.astype(jnp.float32) * projected, axis=1).reshape(
        experts, capacity
    )
    returned = lax.all_to_all(prob_grad, "expert", split_axis=0, concat_axis=0, tiled=True)
    grad_router = returned.reshape(-1)[slot_index].reshape(token_count, top_count)
    scaled = (row_scale[:, None] * slot_rows.astype(jnp.float32)).astype(jnp.bfloat16)
    own_rows = hidden_units // groups
    weight_term = lax.dot_general(
        hidden_rows, scaled, (((0,), (0,)), ((), ())), preferred_element_type=jnp.float32
    )
    weight_term = weight_term.astype(jnp.bfloat16).astype(jnp.float32)
    summed = lax.psum_scatter(
        weight_term.astype(jnp.bfloat16), "dp", scatter_dimension=0, tiled=True
    )
    grad_weight = summed.reshape(1, own_rows, features)
    return (grad_hidden, grad_weight, grad_router)


def solution(mesh):
    placed = (
        P(("expert", "dp"), None),
        P(("expert", "dp"), None),
        P(("expert", "dp"), None),
        P("dp", "expert", None, None, None),
        P("expert", None, None),
    )
    return jax.shard_map(
        on_device,
        mesh=mesh,
        in_specs=placed,
        out_specs=(
            P("dp", "expert", None, None, None),
            P("expert", "dp", None),
            P(("expert", "dp"), None),
        ),
        check_vma=False,
    )
```

profile of v0, /device:TPU:0, one launch (start us, length us, event | category | flops | bytes accessed | tf_op | source)
XLA Modules:
  0.0 111.4 jit_solution(7595150779330000744)
XLA Ops:
  7.2 0.0 copy-start
  7.2 0.7 broadcast_multiply_fusion
  7.9 0.8 copy.17
  8.7 0.1 eq.25
  8.8 0.1 eq.29
  8.8 0.1 copy.16
  8.9 0.1 mul.41
  9.0 0.6 reduce-window.6
  9.6 0.2 slice_reduce_fusion
  9.8 0.8 copy.20
  10.6 0.1 reshape.130
  10.7 0.1 fusion.9
  10.8 2.2 %scatter_custom_fusion = bf16[384]{0:T(512)(128)(2,1)S(1)} fusion(s32[256]{0:T(256)S(1)} %bitcast.47, bf16[256]{0:T(256)(128)(2,1)S(1)} %reshape.130, bf16[]{:T(256)} %constant.5.clone.1), kind=kCustom, calls=%fused_computation.26 | custom fusion | bytes 770 | tf_op jit(solution)/shard_map/scatter | solution.py:27
  13.0 0.7 all_to_all.20
  13.7 8.3 %all-to-all-start = ((bf16[16,1,24]{2,1,0:T(2,128)(2,1)}), bf16[16,1,24]{2,1,0:T(2,128)(2,1)S(1)}, u32[]{:S(2)}, u32[]{:S(2)}) async-start(bf16[16,1,24]{2,1,0:T(2,128)(2,1)} %all_to_all.20), calls=%async_computation | async-start | bytes 16384 | tf_op jit(solution)/shard_map/all_to_all | solution.py:32
  22.0 0.0 copy-done
  22.0 3.2 %scatter_custom_fusion.1 = bf16[384,1792]{1,0:T(8,128)(2,1)} fusion(s32[256]{0:T(256)S(1)} %bitcast.48, bf16[]{:T(256)} %constant.5.clone.1, bf16[32,1792]{1,0:T(8,128)(2,1)S(1)} %copy-done), kind=kCustom, calls=%fused_computation.10 | custom fusion | bytes 1490946 | tf_op jit(solution)/shard_map/scatter | solution.py:21
  25.2 4.0 %all-to-all-done = bf16[16,1,24]{2,1,0:T(2,128)(2,1)S(1)} async-done(((bf16[16,1,24]{2,1,0:T(2,128)(2,1)}), bf16[16,1,24]{2,1,0:T(2,128)(2,1)S(1)}, u32[]{:S(2)}, u32[]{:S(2)}) %all-to-all-start) | async-done | bytes 800 | tf_op jit(solution)/shard_map/all_to_all | solution.py:32
  29.2 3.7 %all-to-all-start.1 = ((bf16[16,24,1792]{2,1,0:T(8,128)(2,1)}), bf16[16,24,1792]{2,1,0:T(8,128)(2,1)S(1)}, u32[]{:S(2)}, u32[]{:S(2)}) async-start(bf16[16,24,1792]{2,1,0:T(8,128)(2,1)} %bitcast.4), calls=%async_computation.1 | async-start | bytes 2752512 | tf_op jit(solution)/shard_map/all_to_all | solution.py:31
  32.9 0.0 copy-start.1
  32.9 0.0 reduce-scatter.4.cloned.1.call-start
  33.0 29.5 %all-to-all-done.1 = bf16[16,24,1792]{2,1,0:T(8,128)(2,1)S(1)} async-done(((bf16[16,24,1792]{2,1,0:T(8,128)(2,1)}), bf16[16,24,1792]{2,1,0:T(8,128)(2,1)S(1)}, u32[]{:S(2)}, u32[]{:S(2)}) %all-to-all-start.1) | async-done | bytes 1376288 | tf_op jit(solution)/shard_map/all_to_all | solution.py:31
  62.5 0.3 multiply_convert_fusion
  62.8 0.0 copy-done.1
  62.8 4.7 %fusion = bf16[1280,1792]{0,1:T(8,128)(2,1)} fusion(bf16[384,1792]{1,0:T(8,128)(2,1)S(1)} %bitcast.45, bf16[384,1280]{1,0:T(8,128)(2,1)S(1)} %bitcast.51), kind=kOutput, calls=%fused_computation.4 | convolution fusion | flops 1763901440 | bytes 6946816 | tf_op jit(solution)/shard_map/dot_general | solution.py:50
  67.5 7.2 %copy.24 = bf16[1280,1792]{1,0:T(8,128)(2,1)} copy(bf16[1280,1792]{0,1:T(8,128)(2,1)} %fusion) | data formatting | bytes 9175040
  74.8 0.0 reduce-scatter.4.cloned.1.call-update
  74.8 0.1 reshape.116
  74.9 5.3 %multiply_reduce_fusion = (f32[384]{0:T(512)S(1)}, bf16[384,1280]{1,0:T(8,128)(2,1)}) fusion(bf16[1,1,16,24,1280]{4,3,2,1,0:T(8,128)(2,1)S(1)} %copy-done.1, f32[384]{0:T(512)S(1)} %reshape.116, bf16[384,1792]{1,0:T(8,128)(2,1)S(1)} %bitcast.44, bf16[1,1280,1792]{2,1,0:T(8,128)(2,1)} %param.9), kind=kOutput, calls=%fused_computation.8 | convolution fusion | flops 1764064896 | bytes 7932928 | tf_op jit(solution)/shard_map/dot_general | solution.py:38
  80.2 0.7 all_to_all.18
  80.9 6.5 %all-to-all-start.2 = ((f32[16,1,24]{2,1,0:T(1,128)}), f32[16,1,24]{2,1,0:T(1,128)S(1)}, u32[]{:S(2)}, u32[]{:S(2)}) async-start(f32[16,1,24]{2,1,0:T(1,128)} %all_to_all.18), calls=%async_computation.2 | async-start | bytes 16384 | tf_op jit(solution)/shard_map/all_to_all | solution.py:46
  87.4 7.2 %all-to-all-done.2 = f32[16,1,24]{2,1,0:T(1,128)S(1)} async-done(((f32[16,1,24]{2,1,0:T(1,128)}), f32[16,1,24]{2,1,0:T(1,128)S(1)}, u32[]{:S(2)}, u32[]{:S(2)}) %all-to-all-start.2) | async-done | bytes 1568 | tf_op jit(solution)/shard_map/all_to_all | solution.py:46
  94.5 0.5 broadcast.64
  95.1 0.7 reduce.9
  95.7 0.1 reshape.114
  95.8 1.9 %gather_fusion = f32[256]{0:T(256)S(1)} fusion(f32[384]{0:T(512)S(1)} %reshape.114, s32[1024]{0:T(1024)S(1)} %pad_clamp_fusion), kind=kCustom, calls=%fused_computation | custom fusion | bytes 3072 | tf_op jit(solution)/shard_map/gather | solution.py:47
  97.8 0.1 reshape.115
  97.9 0.7 copy.23
  98.5 0.0 reduce-scatter.4.cloned.1.call-done
  98.5 3.3 %copy.25 = bf16[640,1792]{0,1:T(8,128)(2,1)S(1)} copy(bf16[640,1792]{1,0:T(8,128)(2,1)} %reduce-scatter.4.cloned.1.call-done) | data formatting | bytes 4587520
  101.8 2.7 %copy.22 = bf16[1,640,1792]{2,1,0:T(8,128)(2,1)} copy(bf16[1,640,1792]{1,2,0:T(8,128)(2,1)S(1)} %bitcast.43) | data formatting | bytes 4587520
  (7 shorter events, 0.1 us)
Async XLA Ops:
  7.2 14.8 %copy-start = (bf16[32,1792]{1,0:T(8,128)(2,1)S(1)}, bf16[32,1792]{1,0:T(8,128)(2,1)}, u32[]{:S(2)}) copy-start(bf16[32,1792]{1,0:T(8,128)(2,1)} %param.5) | copy-start | bytes 344068
  13.7 15.5 %all-to-all-start = ((bf16[16,1,24]{2,1,0:T(2,128)(2,1)}), bf16[16,1,24]{2,1,0:T(2,128)(2,1)S(1)}, u32[]{:S(2)}, u32[]{:S(2)}) async-start(bf16[16,1,24]{2,1,0:T(2,128)(2,1)} %all_to_all.20), calls=%async_computation | async-start | bytes 16384 | tf_op jit(solution)/shard_map/all_to_all | solution.py:32
  29.2 33.3 %all-to-all-start.1 = ((bf16[16,24,1792]{2,1,0:T(8,128)(2,1)}), bf16[16,24,1792]{2,1,0:T(8,128)(2,1)S(1)}, u32[]{:S(2)}, u32[]{:S(2)}) async-start(bf16[16,24,1792]{2,1,0:T(8,128)(2,1)} %bitcast.4), calls=%async_computation.1 | async-start | bytes 2752512 | tf_op jit(solution)/shard_map/all_to_all | solution.py:31
  32.9 29.9 %copy-start.1 = (bf16[1,1,16,24,1280]{4,3,2,1,0:T(8,128)(2,1)S(1)}, bf16[1,1,16,24,1280]{4,3,2,1,0:T(8,128)(2,1)}, u32[]{:S(2)}) copy-start(bf16[1,1,16,24,1280]{4,3,2,1,0:T(8,128)(2,1)} %param.8) | copy-start | bytes 2949124
  32.9 65.6 %reduce-scatter.4.cloned.1.call-start = ((), (), s32[]{:S(2)}) async-start(), calls=%async_computation.4 | async-start | bytes 6881280
  80.9 13.7 %all-to-all-start.2 = ((f32[16,1,24]{2,1,0:T(1,128)}), f32[16,1,24]{2,1,0:T(1,128)S(1)}, u32[]{:S(2)}, u32[]{:S(2)}) async-start(f32[16,1,24]{2,1,0:T(1,128)} %all_to_all.18), calls=%async_computation.2 | async-start | bytes 16384 | tf_op jit(solution)/shard_map/all_to_all | solution.py:46
Sparse Core Ops, SparseCore 0:
  74.9 13.2 reduce-scatter.3
where the time goes:
time: 112 us; the launch traced here: 111 us
  waiting for transfers between devices  40.7 us (36%)
  local copies, waits for them, and re-layouts  25.5 us (23%)
  starting transfers between devices  18.5 us (17%)
  between operations  14.2 us (13%)
  matrix products  10 us (9%)
  other arithmetic  2.45 us (2%)
    all_to_all x1, waiting for transfers between devices, on_device(): lax.all_to_all(outgoing, 'expert', split_axis=0, concat_axis=0, tiled=True)  29.5 us
    unnamed x10, local copies, waits for them, and re-layouts  15.4 us
    all_to_all x1, starting transfers between devices, on_device(): lax.all_to_all(scales_out, 'expert', split_axis=0, concat_axis=0, tiled=T...  8.31 us
    all_to_all x1, waiting for transfers between devices, on_device(): lax.all_to_all(prob_grad, 'expert', split_axis=0, concat_axis=0, tiled=True)  7.18 us
    all_to_all x1, starting transfers between devices, on_device(): lax.all_to_all(prob_grad, 'expert', split_axis=0, concat_axis=0, tiled=True)  6.45 us
    dot_general x1, matrix products, on_device(): lax.dot_general(slot_rows, weight, (((1,), (1,)), ((), ())), preferred_el...  5.28 us
    dot_general x1, matrix products, on_device(): lax.dot_general(hidden_rows, scaled, (((0,), (0,)), ((), ())), preferred_...  4.74 us
    all_to_all x1, waiting for transfers between devices, on_device(): lax.all_to_all(scales_out, 'expert', split_axis=0, concat_axis=0, tiled=T...  4.02 us
  transfers between devices with their start and end apart: 4, of which 3 were waited for; matrix products, arithmetic and copies ran while one was open for 11% of the time, Pallas kernels for 0%

commit v1 on v0

--- a/solution.py
+++ b/solution.py
@@ -1,6 +1,8 @@
 import jax
 import jax.numpy as jnp
 from jax import lax
+from jax.experimental import pallas as pl
+from jax.experimental.pallas import tpu as pltpu
 from jax.sharding import PartitionSpec as P
 
 
@@ -58,7 +60,294 @@
     return (grad_hidden, grad_weight, grad_router)
 
 
+MESH = pl.DeviceIdType.MESH
+META = 128
+TILE = 256
+
+
+def inverse(j):
+    return (j // 4) * 4 + (4 - j % 4) % 4
+
+
+def fused_kernel(
+    ids_ref, rw_ref, go_hbm, hid_hbm, w_hbm,
+    gh_hbm, gw_hbm, gr_ref,
+    tok, hid, wv, x, sc, hid_t, hid_out, gh, gw, msg, ret,
+    go_sem, hid_sem, w_sem, gh_sem, gw_sem,
+    tok_send, tok_recv, hid_send, hid_recv, sc_send, sc_recv, ret_send, ret_recv,
+):
+    f32, bf16 = jnp.float32, jnp.bfloat16
+    tokens, features = go_hbm.shape
+    capacity, hidden_units = hid.shape[1], hid.shape[2]
+    half = hidden_units // 2
+    slots = 8 * capacity
+    rows = 8 * tokens
+    me = lax.axis_index("expert")
+    g = lax.axis_index("dp")
+    stride_a, stride_b = 1 + g, 2 - g
+    step_a = stride_a * (1 - 2 * ((me // stride_a) % 2))
+    step_b = stride_b * (1 - 2 * ((me // stride_b) % 2))
+    base = (me, me + step_a, me + step_b, me + step_a + step_b)
+    source = [lax.rem(base[j // 4] + 16 - 4 * (j % 4), 16) for j in range(16)]
+    next_a, next_b = base[1], base[2]
+
+    load_go = pltpu.make_async_copy(go_hbm, tok.at[pl.ds(0, tokens), pl.ds(0, features)], go_sem)
+    load_go.start()
+    load_hid = []
+    for j in range(16):
+        load_hid.append(pltpu.make_async_copy(hid_hbm.at[source[j]], hid.at[j], hid_sem.at[j]))
+        load_hid[j].start()
+    load_w = pltpu.make_async_copy(w_hbm, wv, w_sem)
+    load_w.start()
+
+    barrier = pltpu.get_barrier_semaphore()
+    for j in range(1, 16):
+        pl.semaphore_signal(barrier, inc=1, device_id=(source[j], g), device_id_type=MESH)
+    pl.semaphore_signal(barrier, inc=1, device_id=(me, 1 - g), device_id_type=MESH)
+
+    ids = ids_ref[...]
+    rw = rw_ref[...].astype(f32)
+    lane = lax.broadcasted_iota(jnp.int32, (tokens, META), 1)
+    expert = lane % 16
+    weight = jnp.zeros((tokens, META), f32)
+    routed = jnp.zeros((tokens, META), f32)
+    for k in range(ids.shape[1]):
+        hit = ids[:, k : k + 1] == expert
+        weight += jnp.where(hit, rw[:, k : k + 1], 0.0)
+        routed += jnp.where(hit, 1.0, 0.0)
+    earlier = lax.broadcasted_iota(jnp.int32, (tokens, tokens), 1) < lax.broadcasted_iota(
+        jnp.int32, (tokens, tokens), 0
+    )
+    rank = jnp.dot(
+        jnp.where(earlier, 1.0, 0.0).astype(bf16), routed.astype(bf16), preferred_element_type=f32
+    )
+    rank = jnp.where(routed > 0.0, rank + 1.0, 0.0)
+    meta = jnp.where(lane < 16, weight, jnp.where(lane < 32, rank, 0.0))
+    tok[pl.ds(0, tokens), pl.ds(features, META)] = meta.astype(bf16)
+    msg[...] = jnp.zeros_like(msg)
+    load_go.wait()
+    pl.semaphore_wait(barrier, 16)
+
+    def send_block(src, dst, device, sem):
+        copy = pltpu.make_async_remote_copy(
+            src_ref=tok.at[pl.ds(src * tokens, tokens)],
+            dst_ref=tok.at[pl.ds(dst * tokens, tokens)],
+            send_sem=tok_send.at[sem],
+            recv_sem=tok_recv.at[dst],
+            device_id=(device, g),
+            device_id_type=MESH,
+        )
+        copy.start()
+        return copy
+
+    copies = [None] * 16
+    copies[4] = send_block(0, 4, next_a, 4)
+    copies[8] = send_block(0, 8, next_b, 8)
+    for d in (1, 3, 2):
+        copies[d] = send_block(0, d, source[inverse(d)], d)
+
+    for j in range(16):
+        load_hid[j].wait()
+
+    def turn(i, carry):
+        at = pl.multiple_of(i * 128, 128)
+        mine = pl.multiple_of(g * half + i * 128, 128)
+        other = pl.multiple_of((1 - g) * half + i * 128, 128)
+        for col, ref in ((other, hid_out), (mine, hid_t)):
+            part = hid[:, :, pl.ds(col, 128)].astype(f32).reshape(2 * slots, 128)
+            ref[pl.ds(at, 128), pl.ds(0, 2 * slots)] = part.T.astype(bf16)
+        return carry
+
+    lax.fori_loop(0, half // 128, turn, 0)
+    swap_hid = pltpu.make_async_remote_copy(
+        src_ref=hid_out,
+        dst_ref=hid_t.at[:, pl.ds(2 * slots, 2 * slots)],
+        send_sem=hid_send,
+        recv_sem=hid_recv,
+        device_id=(me, 1 - g),
+        device_id_type=MESH,
+    )
+    swap_hid.start()
+
+    for d in (1, 3, 2):
+        copies[d].wait_recv()
+        copies[4 + d] = send_block(d, 4 + d, next_a, 4 + d)
+        copies[8 + d] = send_block(d, 8 + d, next_b, 8 + d)
+    for d in (0, 1, 3, 2):
+        copies[4 + d].wait_recv()
+        copies[12 + d] = send_block(4 + d, 12 + d, next_b, 12 + d)
+    load_w.wait()
+
+    back = [None] * 16
+    stores = []
+    swaps = []
+
+    def work(part):
+        at = part * rows
+        lanes = lax.broadcasted_iota(jnp.int32, (rows, META), 1)
+        held = tok[pl.ds(at, rows), pl.ds(features, META)].astype(f32)
+        rank1 = jnp.sum(jnp.where(lanes == me + 16, held, 0.0), axis=1, keepdims=True)
+        row = lax.broadcasted_iota(jnp.int32, (rows, 1), 0)
+        first = ((row // tokens) * capacity).astype(f32)
+        target = jnp.where(rank1 > 0.0, first + rank1 - 1.0, -1.0)
+        eye = lax.broadcasted_iota(jnp.int32, (rows, rows), 0) == lax.broadcasted_iota(
+            jnp.int32, (rows, rows), 1
+        )
+        target = jnp.sum(jnp.where(eye, target, 0.0), axis=0, keepdims=True)
+        slot = lax.broadcasted_iota(jnp.int32, (slots, rows), 0).astype(f32)
+        chosen = slot == target
+        pick = jnp.where(chosen, 1.0, 0.0).astype(bf16)
+        slot_meta = jnp.dot(
+            pick, tok[pl.ds(at, rows), pl.ds(features, META)], preferred_element_type=f32
+        )
+        lanes = lax.broadcasted_iota(jnp.int32, (slots, META), 1)
+        scale = jnp.sum(jnp.where(lanes == me, slot_meta, 0.0), axis=1, keepdims=True)
+        for i in range(features // TILE):
+            cols = pl.ds(i * TILE, TILE)
+            moved = jnp.dot(pick, tok[pl.ds(at, rows), cols], preferred_element_type=f32)
+            x[:, cols] = moved.astype(bf16)
+            sc[pl.ds(part * slots, slots), cols] = (scale * moved).astype(bf16)
+        swap = pltpu.make_async_remote_copy(
+            src_ref=sc.at[pl.ds(part * slots, slots)],
+            dst_ref=sc.at[pl.ds((2 + part) * slots, slots)],
+            send_sem=sc_send.at[part],
+            recv_sem=sc_recv.at[part],
+            device_id=(me, 1 - g),
+            device_id_type=MESH,
+        )
+        swap.start()
+        swaps.append(swap)
+        prob = jnp.zeros((slots, 1), f32)
+        for i in range(hidden_units // TILE):
+            cols = pl.ds(i * TILE, TILE)
+            projected = lax.dot_general(
+                x[...], wv[cols, :], (((1,), (1,)), ((), ())), preferred_element_type=f32
+            )
+            saved = hid[pl.ds(8 * part, 8), :, cols].astype(f32).reshape(slots, TILE)
+            prob += jnp.sum(saved * projected, axis=1, keepdims=True)
+            gh[pl.ds(8 * part, 8), :, cols] = (
+                (scale * projected).reshape(8, capacity, TILE).astype(bf16)
+            )
+        by_token = jnp.sum(jnp.where(chosen, prob, 0.0), axis=0, keepdims=True)
+        for i in range(8):
+            j = 8 * part + i
+            mine = by_token[:, tokens * i : tokens * (i + 1)]
+            if j == 0:
+                ret[0, 0:1, 0:tokens] = mine
+            else:
+                msg[j, 0:1, 0:tokens] = mine
+        for i in range(8):
+            j = 8 * part + i
+            if j > 0:
+                back[j] = pltpu.make_async_remote_copy(
+                    src_ref=msg.at[j],
+                    dst_ref=ret.at[inverse(j)],
+                    send_sem=ret_send.at[j],
+                    recv_sem=ret_recv.at[inverse(j)],
+                    device_id=(source[j], g),
+                    device_id_type=MESH,
+                )
+                back[j].start()
+        for i in range(8):
+            j = 8 * part + i
+            store = pltpu.make_async_copy(gh.at[j], gh_hbm.at[source[j]], gh_sem.at[j])
+            store.start()
+            stores.append(store)
+
+    work(0)
+    for j in (8, 9, 11, 10, 12, 13, 15, 14):
+        copies[j].wait_recv()
+    work(1)
+
+    swap_hid.wait_recv()
+    for swap in swaps:
+        swap.wait_recv()
+    for i in range(features // TILE):
+        cols = pl.ds(i * TILE, TILE)
+        gw[:, cols] = jnp.dot(hid_t[...], sc[:, cols], preferred_element_type=f32).astype(bf16)
+        store = pltpu.make_async_copy(gw.at[:, cols], gw_hbm.at[:, cols], gw_sem.at[i])
+        store.start()
+        stores.append(store)
+
+    eye = lax.broadcasted_iota(jnp.int32, (tokens, tokens), 0) == lax.broadcasted_iota(
+        jnp.int32, (tokens, tokens), 1
+    )
+    total = jnp.zeros(ids.shape, f32)
+    for j in range(16):
+        if j > 0:
+            back[inverse(j)].wait_recv()
+        column = jnp.sum(jnp.where(eye, ret[j, 0:1, 0:tokens], 0.0), axis=1, keepdims=True)
+        total += jnp.where(ids == source[j], column, 0.0)
+    gr_ref[...] = total
+
+    for j in range(1, 16):
+        copies[j].wait_send()
+        back[j].wait_send()
+    swap_hid.wait_send()
+    for swap in swaps:
+        swap.wait_send()
+    for store in stores:
+        store.wait()
+
+
+def on_pair(grad_out, expert_ids, router_weights, saved_hidden, down_weight):
+    tokens, features = grad_out.shape
+    _, _, experts, capacity, hidden_units = saved_hidden.shape
+    half = hidden_units // 2
+    slots = experts * capacity
+    bf16, f32 = jnp.bfloat16, jnp.float32
+    dma = pltpu.SemaphoreType.DMA
+    vmem = pl.BlockSpec(memory_space=pltpu.VMEM)
+    hbm = pl.BlockSpec(memory_space=pl.ANY)
+    grad_hidden, grad_weight, grad_router = pl.pallas_call(
+        fused_kernel,
+        out_shape=(
+            jax.ShapeDtypeStruct((experts, capacity, hidden_units), bf16),
+            jax.ShapeDtypeStruct((half, features), bf16),
+            jax.ShapeDtypeStruct(expert_ids.shape, f32),
+        ),
+        in_specs=[vmem, vmem, hbm, hbm, hbm],
+        out_specs=(hbm, hbm, vmem),
+        scratch_shapes=[
+            pltpu.VMEM((experts * tokens, features + META), bf16),
+            pltpu.VMEM((experts, capacity, hidden_units), bf16),
+            pltpu.VMEM((hidden_units, features), bf16),
+            pltpu.VMEM((slots // 2, features), bf16),
+            pltpu.VMEM((2 * slots, features), bf16),
+            pltpu.VMEM((half, 2 * slots), bf16),
+            pltpu.VMEM((half, slots), bf16),
+            pltpu.VMEM((experts, capacity, hidden_units), bf16),
+            pltpu.VMEM((half, features), bf16),
+            pltpu.VMEM((experts, 8, 128), f32),
+            pltpu.VMEM((experts, 8, 128), f32),
+            dma,
+            dma((16,)),
+            dma,
+            dma((16,)),
+            dma((features // TILE,)),
+            dma((16,)),
+            dma((16,)),
+            dma,
+            dma,
+            dma((2,)),
+            dma((2,)),
+            dma((16,)),
+            dma((16,)),
+        ],
+        compiler_params=pltpu.CompilerParams(
+            collective_id=0, has_side_effects=True, vmem_limit_bytes=48 * 1024 * 1024
+        ),
+        cost_estimate=pl.CostEstimate(
+            flops=4 * slots * hidden_units * features,
+            bytes_accessed=10_000_000,
+            transcendentals=0,
+        ),
+    )(expert_ids, router_weights, grad_out, saved_hidden[0, 0], down_weight[0])
+    return grad_hidden[None, None], grad_weight[None], grad_router
+
+
 def solution(mesh):
+    fused = mesh.shape["expert"] == 16 and mesh.shape["dp"] == 2
     placed = (
         P(("expert", "dp"), None),
         P(("expert", "dp"), None),
@@ -67,7 +356,7 @@
         P("expert", None, None),
     )
     return jax.shard_map(
-        on_device,
+        on_pair if fused else on_device,
         mesh=mesh,
         in_specs=placed,
         out_specs=(

time: 112 us -> 48.1 us (0.43)
  waiting for transfers between devices: 40.7 us -> 0 us
  Pallas kernels: 0 us -> 40.6 us
  local copies, waits for them, and re-layouts: 25.5 us -> 6.62 us
  starting transfers between devices: 18.5 us -> 0 us
  between operations: 14.2 us -> 0.64 us
  matrix products: 10 us -> 0 us
  other arithmetic: 2.45 us -> 0 us
    all_to_all x3 -> x0, waiting for transfers between devices: 40.7 us -> none  [the longest x1 29.5 us: on_device(): lax.all_to_all(outgoing, 'expert', split_axis=0, concat_axis=0, tiled=True)]
    pallas_call x0 -> x1, Pallas kernels: none -> 40.6 us  [on_pair(): pl.pallas_call(fused_kernel, out_shape=(jax.ShapeDtypeStruct((experts, ca...]
    all_to_all x3 -> x0, starting transfers between devices: 18.5 us -> none  [the longest x1 8.31 us: on_device(): lax.all_to_all(scales_out, 'expert', split_axis=0, concat_axis=0, tiled=T...]
    dot_general x2 -> x0, matrix products: 10 us -> none  [the longest x1 5.28 us: on_device(): lax.dot_general(slot_rows, weight, (((1,), (1,)), ((), ())), preferred_el...]
    unnamed x10 -> x9, local copies, waits for them, and re-layouts: 15.4 us -> 6.62 us
    scatter x2 -> x0, local copies, waits for them, and re-layouts: 5.33 us -> none  [the longest x1 3.17 us: on_device(): jnp.zeros((experts * capacity, features), jnp.bfloat16).at[slot_index]]
    gather x1 -> x0, local copies, waits for them, and re-layouts: 1.95 us -> none  [on_device(): returned.reshape(-1)[slot_index].reshape(token_count, top_count)]
    all_to_all x3 -> x0, local copies, waits for them, and re-layouts: 1.91 us -> none  [the longest x2 1.21 us: on_device(): lax.all_to_all(prob_grad, 'expert', split_axis=0, concat_axis=0, tiled=True)]
  transfers between devices with their start and end apart: 4 -> 0, of which waited for: 3 -> 0; matrix products, arithmetic and copies ran while one was open for 11% -> 0% of each run, Pallas kernels for 0% -> 0%
where the time goes in v1:
time: 48.1 us; the launch traced here: 47.9 us
  Pallas kernels  40.6 us (84%)
  local copies, waits for them, and re-layouts  6.62 us (14%)
  between operations  0.64 us (1%)
    pallas_call x1, Pallas kernels, on_pair(): pl.pallas_call(fused_kernel, out_shape=(jax.ShapeDtypeStruct((experts, ca...  40.6 us
    unnamed x9, local copies, waits for them, and re-layouts  6.62 us

profile of v1, /device:TPU:0, one launch (start us, length us, event | category | flops | bytes accessed | tf_op | source)
XLA Modules:
  0.0 47.9 jit_solution(1637557172187868927)
XLA Ops:
  0.6 0.8 %copy.9.rw_ref = bf16[32,8]{1,0:T(8,128)(2,1)S(1)} copy(bf16[32,8]{0,1:T(8,128)(2,1)} %param.7) | data formatting | bytes 1024 | tf_op args[2]
  1.4 0.8 %copy.8.ids_ref = s32[32,8]{1,0:T(8,128)S(1)} copy(s32[32,8]{0,1:T(8,128)} %param.6) | data formatting | bytes 2048 | tf_op args[1]
  2.2 0.0 copy-start
  2.2 1.2 %copy-done = bf16[1,1,16,24,1280]{4,3,2,1,0:T(8,128)(2,1)S(1)} copy-done((bf16[1,1,16,24,1280]{4,3,2,1,0:T(8,128)(2,1)S(1)}, bf16[1,1,16,24,1280]{4,3,2,1,0:T(8,128)(2,1)}, u32[]{:S(2)}) %copy-start) | copy-done | bytes 983064
  3.4 0.0 copy-start.1
  3.4 0.9 %copy-done.1 = bf16[32,1792]{1,0:T(8,128)(2,1)S(1)} copy-done((bf16[32,1792]{1,0:T(8,128)(2,1)S(1)}, bf16[32,1792]{1,0:T(8,128)(2,1)}, u32[]{:S(2)}) %copy-start.1) | copy-done | bytes 114712
  4.3 40.6 %shard_map.76 = (bf16[16,24,1280]{2,1,0:T(8,128)(2,1)S(1)}, bf16[640,1792]{1,0:T(8,128)(2,1)S(1)}, f32[32,8]{1,0:T(8,128)S(1)}) custom-call(s32[32,8]{1,0:T(8,128)S(1)} %copy.8.ids_ref, bf16[32,8]{1,0:T(8,128)(2,1)S(1)} %copy.9.rw_ref, bf16[32,1792]{1,0:T(8,128)(2,1)S(1)} %copy-done.1, bf16[16,24,1280]{2,1,0:T(8,128)(2,1)S(1)} %bitcast.6, ...), custom_call_target="tpu_custom_call" | custom-call | flops 3523215360 | bytes 10000000 | tf_op jit(solution)/shard_map/pallas_call | solution.py:302
  44.9 0.7 %copy.10 = f32[32,8]{0,1:T(8,128)} copy(f32[32,8]{1,0:T(8,128)S(1)} %get-tuple-element.11) | data formatting | bytes 2048
  45.6 0.9 %copy.13 = bf16[1,1,16,24,1280]{4,3,2,1,0:T(8,128)(2,1)} copy(bf16[1,1,16,24,1280]{4,3,2,1,0:T(8,128)(2,1)S(1)} %bitcast.5) | data formatting | bytes 1966080
  46.5 1.4 %copy.14 = bf16[1,640,1792]{2,1,0:T(8,128)(2,1)} copy(bf16[1,640,1792]{2,1,0:T(8,128)(2,1)S(1)} %bitcast.4) | data formatting | bytes 4587520
Async XLA Ops:
  2.2 1.2 %copy-start = (bf16[1,1,16,24,1280]{4,3,2,1,0:T(8,128)(2,1)S(1)}, bf16[1,1,16,24,1280]{4,3,2,1,0:T(8,128)(2,1)}, u32[]{:S(2)}) copy-start(bf16[1,1,16,24,1280]{4,3,2,1,0:T(8,128)(2,1)} %param.8) | copy-start | bytes 2949124
  3.4 0.9 %copy-start.1 = (bf16[32,1792]{1,0:T(8,128)(2,1)S(1)}, bf16[32,1792]{1,0:T(8,128)(2,1)}, u32[]{:S(2)}) copy-start(bf16[32,1792]{1,0:T(8,128)(2,1)} %go_hbm.1) | copy-start | bytes 344068

commit v2 on v1

--- a/solution.py
+++ b/solution.py
@@ -72,9 +72,9 @@
 def fused_kernel(
     ids_ref, rw_ref, go_hbm, hid_hbm, w_hbm,
     gh_hbm, gw_hbm, gr_ref,
-    tok, hid, wv, x, sc, hid_t, hid_out, gh, gw, msg, ret,
+    tok, hid, wv, x, sc, hid_own, hid_sib, hid_out, acc, gh, gw, msg, ret,
     go_sem, hid_sem, w_sem, gh_sem, gw_sem,
-    tok_send, tok_recv, hid_send, hid_recv, sc_send, sc_recv, ret_send, ret_recv,
+    tok_send, tok_recv, z_send, hid_send, hid_recv, sc_send, sc_recv, ret_send, ret_recv,
 ):
     f32, bf16 = jnp.float32, jnp.bfloat16
     tokens, features = go_hbm.shape
@@ -91,6 +91,11 @@
     source = [lax.rem(base[j // 4] + 16 - 4 * (j % 4), 16) for j in range(16)]
     next_a, next_b = base[1], base[2]
 
+    barrier = pltpu.get_barrier_semaphore()
+    for j in range(1, 16):
+        pl.semaphore_signal(barrier, inc=1, device_id=(source[j], g), device_id_type=MESH)
+    pl.semaphore_signal(barrier, inc=1, device_id=(me, 1 - g), device_id_type=MESH)
+
     load_go = pltpu.make_async_copy(go_hbm, tok.at[pl.ds(0, tokens), pl.ds(0, features)], go_sem)
     load_go.start()
     load_hid = []
@@ -100,51 +105,75 @@
     load_w = pltpu.make_async_copy(w_hbm, wv, w_sem)
     load_w.start()
 
-    barrier = pltpu.get_barrier_semaphore()
-    for j in range(1, 16):
-        pl.semaphore_signal(barrier, inc=1, device_id=(source[j], g), device_id_type=MESH)
-    pl.semaphore_signal(barrier, inc=1, device_id=(me, 1 - g), device_id_type=MESH)
-
     ids = ids_ref[...]
     rw = rw_ref[...].astype(f32)
-    lane = lax.broadcasted_iota(jnp.int32, (tokens, META), 1)
-    expert = lane % 16
-    weight = jnp.zeros((tokens, META), f32)
-    routed = jnp.zeros((tokens, META), f32)
-    for k in range(ids.shape[1]):
-        hit = ids[:, k : k + 1] == expert
-        weight += jnp.where(hit, rw[:, k : k + 1], 0.0)
+    place = lax.broadcasted_iota(jnp.int32, (META, tokens), 0)
+    expert = place % 16
+    weight = jnp.zeros((META, tokens), f32)
+    routed = jnp.zeros((META, tokens), f32)
+    for k in range(ids.shape[0]):
+        hit = ids[k : k + 1, :] == expert
+        weight += jnp.where(hit, rw[k : k + 1, :], 0.0)
         routed += jnp.where(hit, 1.0, 0.0)
-    earlier = lax.broadcasted_iota(jnp.int32, (tokens, tokens), 1) < lax.broadcasted_iota(
-        jnp.int32, (tokens, tokens), 0
-    )
+    one = lax.broadcasted_iota(jnp.int32, (tokens, tokens), 0)
+    two = lax.broadcasted_iota(jnp.int32, (tokens, tokens), 1)
     rank = jnp.dot(
-        jnp.where(earlier, 1.0, 0.0).astype(bf16), routed.astype(bf16), preferred_element_type=f32
+        routed.astype(bf16), jnp.where(one < two, 1.0, 0.0).astype(bf16), preferred_element_type=f32
     )
     rank = jnp.where(routed > 0.0, rank + 1.0, 0.0)
-    meta = jnp.where(lane < 16, weight, jnp.where(lane < 32, rank, 0.0))
+    meta = jnp.where(place < 16, weight, jnp.where(place < 32, rank, 0.0))
+    meta = lax.dot_general(
+        jnp.where(one == two, 1.0, 0.0).astype(bf16),
+        meta.astype(bf16),
+        (((1,), (1,)), ((), ())),
+        preferred_element_type=f32,
+    )
     tok[pl.ds(0, tokens), pl.ds(features, META)] = meta.astype(bf16)
     msg[...] = jnp.zeros_like(msg)
     load_go.wait()
     pl.semaphore_wait(barrier, 16)
 
-    def send_block(src, dst, device, sem):
-        copy = pltpu.make_async_remote_copy(
-            src_ref=tok.at[pl.ds(src * tokens, tokens)],
-            dst_ref=tok.at[pl.ds(dst * tokens, tokens)],
-            send_sem=tok_send.at[sem],
+    def block(src, dst, device, sem):
+        return pltpu.make_async_remote_copy(
+            src_ref=tok.at[pl.ds(pl.multiple_of(src * tokens, tokens), tokens)],
+            dst_ref=tok.at[pl.ds(pl.multiple_of(dst * tokens, tokens), tokens)],
+            send_sem=sem,
             recv_sem=tok_recv.at[dst],
             device_id=(device, g),
             device_id_type=MESH,
         )
-        copy.start()
-        return copy
-
-    copies = [None] * 16
-    copies[4] = send_block(0, 4, next_a, 4)
-    copies[8] = send_block(0, 8, next_b, 8)
-    for d in (1, 3, 2):
-        copies[d] = send_block(0, d, source[inverse(d)], d)
+
+    def over_a(d):
+        return block(d, 4 + d, next_a, tok_send.at[4 + d])
+
+    def over_b(j):
+        return block(j, 8 + j, next_b, tok_send.at[8 + j])
+
+    z = me // 4
+    first, last = 1 - (z + 3) // 4, z // 3
+    order = (1 + 2 * first, 3 - first - last, 2 + last - first)
+
+    def along_z(act):
+        @pl.when(z < 3)
+        def _():
+            act(block(0, 1, me + 4, z_send.at[0]))
+
+        @pl.when(z > 0)
+        def _():
+            act(block(0, 3, me - 4, z_send.at[4]))
+
+    def pass_on(d, act):
+        @pl.when(jnp.logical_and(d <= z, z < 3))
+        def _():
+            act(block(d, d + 1, me + 4, z_send.at[d]))
+
+        @pl.when(jnp.logical_and(d > z, z > 0))
+        def _():
+            act(block(d, d - 1, me - 4, z_send.at[d]))
+
+    along_z(lambda copy: copy.start())
+    over_a(0).start()
+    over_b(0).start()
 
     for j in range(16):
         load_hid[j].wait()
@@ -153,15 +182,16 @@
         at = pl.multiple_of(i * 128, 128)
         mine = pl.multiple_of(g * half + i * 128, 128)
         other = pl.multiple_of((1 - g) * half + i * 128, 128)
-        for col, ref in ((other, hid_out), (mine, hid_t)):
-            part = hid[:, :, pl.ds(col, 128)].astype(f32).reshape(2 * slots, 128)
-            ref[pl.ds(at, 128), pl.ds(0, 2 * slots)] = part.T.astype(bf16)
+        for part in range(2):
+            for col, ref in ((other, hid_out), (mine, hid_own)):
+                piece = hid[pl.ds(8 * part, 8), :, pl.ds(col, 128)].astype(f32).reshape(slots, 128)
+                ref[part, pl.ds(at, 128), :] = piece.T.astype(bf16)
         return carry
 
     lax.fori_loop(0, half // 128, turn, 0)
     swap_hid = pltpu.make_async_remote_copy(
         src_ref=hid_out,
-        dst_ref=hid_t.at[:, pl.ds(2 * slots, 2 * slots)],
+        dst_ref=hid_sib,
         send_sem=hid_send,
         recv_sem=hid_recv,
         device_id=(me, 1 - g),
@@ -169,13 +199,17 @@
     )
     swap_hid.start()
 
-    for d in (1, 3, 2):
-        copies[d].wait_recv()
-        copies[4 + d] = send_block(d, 4 + d, next_a, 4 + d)
-        copies[8 + d] = send_block(d, 8 + d, next_b, 8 + d)
-    for d in (0, 1, 3, 2):
-        copies[4 + d].wait_recv()
-        copies[12 + d] = send_block(4 + d, 12 + d, next_b, 12 + d)
+    before = 0
+    for d in order:
+        block(0, d, next_a, tok_send.at[0]).wait_recv()
+        pass_on(d, lambda copy: copy.start())
+        over_a(d).start()
+        over_b(d).start()
+        over_a(before).wait_recv()
+        over_b(4 + before).start()
+        before = d
+    over_a(before).wait_recv()
+    over_b(4 + before).start()
     load_w.wait()
 
     back = [None] * 16
@@ -254,34 +288,45 @@
             store.start()
             stores.append(store)
 
+    def weight_part(part, cols):
+        return jnp.dot(
+            hid_own[part], sc[pl.ds(part * slots, slots), cols], preferred_element_type=f32
+        ) + jnp.dot(
+            hid_sib[part], sc[pl.ds((2 + part) * slots, slots), cols], preferred_element_type=f32
+        )
+
     work(0)
-    for j in (8, 9, 11, 10, 12, 13, 15, 14):
-        copies[j].wait_recv()
-    work(1)
-
     swap_hid.wait_recv()
-    for swap in swaps:
-        swap.wait_recv()
+    swaps[0].wait_recv()
     for i in range(features // TILE):
         cols = pl.ds(i * TILE, TILE)
-        gw[:, cols] = jnp.dot(hid_t[...], sc[:, cols], preferred_element_type=f32).astype(bf16)
+        acc[:, cols] = weight_part(0, cols)
+    for j in range(8):
+        over_b(j).wait_recv()
+    work(1)
+    swaps[1].wait_recv()
+    for i in range(features // TILE):
+        cols = pl.ds(i * TILE, TILE)
+        gw[:, cols] = (acc[:, cols] + weight_part(1, cols)).astype(bf16)
         store = pltpu.make_async_copy(gw.at[:, cols], gw_hbm.at[:, cols], gw_sem.at[i])
         store.start()
         stores.append(store)
 
-    eye = lax.broadcasted_iota(jnp.int32, (tokens, tokens), 0) == lax.broadcasted_iota(
-        jnp.int32, (tokens, tokens), 1
-    )
     total = jnp.zeros(ids.shape, f32)
     for j in range(16):
         if j > 0:
             back[inverse(j)].wait_recv()
-        column = jnp.sum(jnp.where(eye, ret[j, 0:1, 0:tokens], 0.0), axis=1, keepdims=True)
-        total += jnp.where(ids == source[j], column, 0.0)
+        total += jnp.where(ids == source[j], ret[j, 0:1, 0:tokens], 0.0)
     gr_ref[...] = total
 
+    along_z(lambda copy: copy.wait_send())
+    for d in order:
+        pass_on(d, lambda copy: copy.wait_send())
+    for d in range(4):
+        over_a(d).wait_send()
+    for j in range(8):
+        over_b(j).wait_send()
     for j in range(1, 16):
-        copies[j].wait_send()
         back[j].wait_send()
     swap_hid.wait_send()
     for swap in swaps:
@@ -304,7 +349,7 @@
         out_shape=(
             jax.ShapeDtypeStruct((experts, capacity, hidden_units), bf16),
             jax.ShapeDtypeStruct((half, features), bf16),
-            jax.ShapeDtypeStruct(expert_ids.shape, f32),
+            jax.ShapeDtypeStruct(expert_ids.shape[::-1], f32),
         ),
         in_specs=[vmem, vmem, hbm, hbm, hbm],
         out_specs=(hbm, hbm, vmem),
@@ -314,8 +359,10 @@
             pltpu.VMEM((hidden_units, features), bf16),
             pltpu.VMEM((slots // 2, features), bf16),
             pltpu.VMEM((2 * slots, features), bf16),
-            pltpu.VMEM((half, 2 * slots), bf16),
-            pltpu.VMEM((half, slots), bf16),
+            pltpu.VMEM((2, half, slots // 2), bf16),
+            pltpu.VMEM((2, half, slots // 2), bf16),
+            pltpu.VMEM((2, half, slots // 2), bf16),
+            pltpu.VMEM((half, features), f32),
             pltpu.VMEM((experts, capacity, hidden_units), bf16),
             pltpu.VMEM((half, features), bf16),
             pltpu.VMEM((experts, 8, 128), f32),
@@ -327,6 +374,7 @@
             dma((features // TILE,)),
             dma((16,)),
             dma((16,)),
+            dma((5,)),
             dma,
             dma,
             dma((2,)),
@@ -335,15 +383,15 @@
             dma((16,)),
         ],
         compiler_params=pltpu.CompilerParams(
-            collective_id=0, has_side_effects=True, vmem_limit_bytes=48 * 1024 * 1024
+            collective_id=0, has_side_effects=True, vmem_limit_bytes=58 * 1024 * 1024
         ),
         cost_estimate=pl.CostEstimate(
             flops=4 * slots * hidden_units * features,
             bytes_accessed=10_000_000,
             transcendentals=0,
         ),
-    )(expert_ids, router_weights, grad_out, saved_hidden[0, 0], down_weight[0])
-    return grad_hidden[None, None], grad_weight[None], grad_router
+    )(expert_ids.T, router_weights.T, grad_out, saved_hidden[0, 0], down_weight[0])
+    return grad_hidden[None, None], grad_weight[None], grad_router.T
 
 
 def solution(mesh):

time: 48.1 us -> 44.2 us (0.919)
  Pallas kernels: 40.6 us -> 37.3 us
  local copies, waits for them, and re-layouts: 6.62 us -> 5.98 us
    pallas_call x1, Pallas kernels: 40.6 us -> 37.3 us  [on_pair(): pl.pallas_call(fused_kernel, out_shape=(jax.ShapeDtypeStruct((experts, ca...]
    unnamed x9 -> x5, local copies, waits for them, and re-layouts: 6.62 us -> 5.98 us
where the time goes in v2:
time: 44.2 us; the launch traced here: 43.9 us
  Pallas kernels  37.3 us (84%)
  local copies, waits for them, and re-layouts  5.98 us (14%)
  between operations  0.64 us (1%)
    pallas_call x1, Pallas kernels, on_pair(): pl.pallas_call(fused_kernel, out_shape=(jax.ShapeDtypeStruct((experts, ca...  37.3 us
    unnamed x5, local copies, waits for them, and re-layouts  5.98 us

profile of v2, /device:TPU:0, one launch (start us, length us, event | category | flops | bytes accessed | tf_op | source)
XLA Modules:
  0.0 43.9 jit_solution(6417400120362613856)
XLA Ops:
  0.6 37.3 %shard_map.76 = (bf16[16,24,1280]{2,1,0:T(8,128)(2,1)}, bf16[640,1792]{1,0:T(8,128)(2,1)}, f32[8,32]{1,0:T(8,128)}) custom-call(s32[8,32]{1,0:T(8,128)} %bitcast.12, bf16[8,32]{1,0:T(8,128)(2,1)} %bitcast.13, bf16[32,1792]{1,0:T(8,128)(2,1)} %go_hbm.1, bf16[16,24,1280]{2,1,0:T(8,128)(2,1)} %bitcast.11, bf16[1280,1792]{1,0:T(8,128)(2,1)} %bitcast.10), custom_call_target="tpu_custom_call" | custom-call | flops 3523215360 | bytes 10000000 | tf_op jit(solution)/shard_map/pallas_call | solution.py:347
  37.9 2.2 %copy.11 = bf16[1,1,16,24,1280]{4,3,2,1,0:T(8,128)(2,1)} copy(bf16[1,1,16,24,1280]{4,3,2,1,0:T(8,128)(2,1)} %bitcast.8) | data formatting | bytes 1966080
  40.2 0.0 copy-start
  40.2 3.2 %copy.12 = bf16[1,640,1792]{2,1,0:T(8,128)(2,1)} copy(bf16[1,640,1792]{2,1,0:T(8,128)(2,1)} %bitcast.7) | data formatting | bytes 4587520
  43.3 0.0 copy-done
  43.3 0.6 %copy.13 = f32[32,8]{0,1:T(8,128)} copy(f32[32,8]{0,1:T(8,128)S(1)} %bitcast.9) | data formatting | bytes 2048
Async XLA Ops:
  40.2 3.2 %copy-start = (f32[8,32]{1,0:T(8,128)S(1)}, f32[8,32]{1,0:T(8,128)}, u32[]{:S(2)}) copy-start(f32[8,32]{1,0:T(8,128)} %get-tuple-element.8) | copy-start | bytes 3076

commit v3 on v2

--- a/solution.py
+++ b/solution.py
@@ -71,9 +71,9 @@
 
 def fused_kernel(
     ids_ref, rw_ref, go_hbm, hid_hbm, w_hbm,
-    gh_hbm, gw_hbm, gr_ref,
-    tok, hid, wv, x, sc, hid_own, hid_sib, hid_out, acc, gh, gw, msg, ret,
-    go_sem, hid_sem, w_sem, gh_sem, gw_sem,
+    gh, gw, gr_ref,
+    tok, hid, wv, x, sc, hid_own, hid_sib, hid_out, acc, msg, ret,
+    go_sem, hid_sem, w_sem,
     tok_send, tok_recv, z_send, hid_send, hid_recv, sc_send, sc_recv, ret_send, ret_recv,
 ):
     f32, bf16 = jnp.float32, jnp.bfloat16
@@ -133,47 +133,50 @@
     load_go.wait()
     pl.semaphore_wait(barrier, 16)
 
-    def block(src, dst, device, sem):
+    part_rows = tokens // 2
+
+    def block(src, dst, device, send, p):
         return pltpu.make_async_remote_copy(
-            src_ref=tok.at[pl.ds(pl.multiple_of(src * tokens, tokens), tokens)],
-            dst_ref=tok.at[pl.ds(pl.multiple_of(dst * tokens, tokens), tokens)],
-            send_sem=sem,
-            recv_sem=tok_recv.at[dst],
+            src_ref=tok.at[pl.ds(pl.multiple_of(src * tokens + p * part_rows, part_rows), part_rows)],
+            dst_ref=tok.at[pl.ds(pl.multiple_of(dst * tokens + p * part_rows, part_rows), part_rows)],
+            send_sem=send.at[p],
+            recv_sem=tok_recv.at[dst, p],
             device_id=(device, g),
             device_id_type=MESH,
         )
 
-    def over_a(d):
-        return block(d, 4 + d, next_a, tok_send.at[4 + d])
-
-    def over_b(j):
-        return block(j, 8 + j, next_b, tok_send.at[8 + j])
+    def over_a(d, p):
+        return block(d, 4 + d, next_a, tok_send.at[4 + d], p)
+
+    def over_b(j, p):
+        return block(j, 8 + j, next_b, tok_send.at[8 + j], p)
 
     z = me // 4
     first, last = 1 - (z + 3) // 4, z // 3
     order = (1 + 2 * first, 3 - first - last, 2 + last - first)
 
-    def along_z(act):
+    def along_z(act, p):
         @pl.when(z < 3)
         def _():
-            act(block(0, 1, me + 4, z_send.at[0]))
+            act(block(0, 1, me + 4, z_send.at[0], p))
 
         @pl.when(z > 0)
         def _():
-            act(block(0, 3, me - 4, z_send.at[4]))
-
-    def pass_on(d, act):
+            act(block(0, 3, me - 4, z_send.at[4], p))
+
+    def pass_on(d, act, p):
         @pl.when(jnp.logical_and(d <= z, z < 3))
         def _():
-            act(block(d, d + 1, me + 4, z_send.at[d]))
+            act(block(d, d + 1, me + 4, z_send.at[d], p))
 
         @pl.when(jnp.logical_and(d > z, z > 0))
         def _():
-            act(block(d, d - 1, me - 4, z_send.at[d]))
-
-    along_z(lambda copy: copy.start())
-    over_a(0).start()
-    over_b(0).start()
+            act(block(d, d - 1, me - 4, z_send.at[d], p))
+
+    for p in range(2):
+        along_z(lambda copy: copy.start(), p)
+        over_a(0, p).start()
+        over_b(0, p).start()
 
     for j in range(16):
         load_hid[j].wait()
@@ -201,19 +204,20 @@
 
     before = 0
     for d in order:
-        block(0, d, next_a, tok_send.at[0]).wait_recv()
-        pass_on(d, lambda copy: copy.start())
-        over_a(d).start()
-        over_b(d).start()
-        over_a(before).wait_recv()
-        over_b(4 + before).start()
+        for p in range(2):
+            block(0, d, next_a, tok_send.at[0], p).wait_recv()
+            pass_on(d, lambda copy: copy.start(), p)
+            over_a(d, p).start()
+            over_b(d, p).start()
+            over_a(before, p).wait_recv()
+            over_b(4 + before, p).start()
         before = d
-    over_a(before).wait_recv()
-    over_b(4 + before).start()
+    for p in range(2):
+        over_a(before, p).wait_recv()
+        over_b(4 + before, p).start()
     load_w.wait()
 
     back = [None] * 16
-    stores = []
     swaps = []
 
     def work(part):
@@ -259,9 +263,9 @@
             )
             saved = hid[pl.ds(8 * part, 8), :, cols].astype(f32).reshape(slots, TILE)
             prob += jnp.sum(saved * projected, axis=1, keepdims=True)
-            gh[pl.ds(8 * part, 8), :, cols] = (
-                (scale * projected).reshape(8, capacity, TILE).astype(bf16)
-            )
+            rows_out = (scale * projected).reshape(8, capacity, TILE).astype(bf16)
+            for k in range(8):
+                gh[source[8 * part + k], :, cols] = rows_out[k]
         by_token = jnp.sum(jnp.where(chosen, prob, 0.0), axis=0, keepdims=True)
         for i in range(8):
             j = 8 * part + i
@@ -282,11 +286,6 @@
                     device_id_type=MESH,
                 )
                 back[j].start()
-        for i in range(8):
-            j = 8 * part + i
-            store = pltpu.make_async_copy(gh.at[j], gh_hbm.at[source[j]], gh_sem.at[j])
-            store.start()
-            stores.append(store)
 
     def weight_part(part, cols):
         return jnp.dot(
@@ -302,15 +301,13 @@
         cols = pl.ds(i * TILE, TILE)
         acc[:, cols] = weight_part(0, cols)
     for j in range(8):
-        over_b(j).wait_recv()
+        for p in range(2):
+            over_b(j, p).wait_recv()
     work(1)
     swaps[1].wait_recv()
     for i in range(features // TILE):
         cols = pl.ds(i * TILE, TILE)
         gw[:, cols] = (acc[:, cols] + weight_part(1, cols)).astype(bf16)
-        store = pltpu.make_async_copy(gw.at[:, cols], gw_hbm.at[:, cols], gw_sem.at[i])
-        store.start()
-        stores.append(store)
 
     total = jnp.zeros(ids.shape, f32)
     for j in range(16):
@@ -319,20 +316,19 @@
         total += jnp.where(ids == source[j], ret[j, 0:1, 0:tokens], 0.0)
     gr_ref[...] = total
 
-    along_z(lambda copy: copy.wait_send())
-    for d in order:
-        pass_on(d, lambda copy: copy.wait_send())
-    for d in range(4):
-        over_a(d).wait_send()
-    for j in range(8):
-        over_b(j).wait_send()
+    for p in range(2):
+        along_z(lambda copy: copy.wait_send(), p)
+        for d in order:
+            pass_on(d, lambda copy: copy.wait_send(), p)
+        for d in range(4):
+            over_a(d, p).wait_send()
+        for j in range(8):
+            over_b(j, p).wait_send()
     for j in range(1, 16):
         back[j].wait_send()
     swap_hid.wait_send()
     for swap in swaps:
         swap.wait_send()
-    for store in stores:
-        store.wait()
 
 
 def on_pair(grad_out, expert_ids, router_weights, saved_hidden, down_weight):
@@ -351,8 +347,8 @@
             jax.ShapeDtypeStruct((half, features), bf16),
             jax.ShapeDtypeStruct(expert_ids.shape[::-1], f32),
         ),
-        in_specs=[vmem, vmem, hbm, hbm, hbm],
-        out_specs=(hbm, hbm, vmem),
+        in_specs=[vmem, vmem] + [pl.BlockSpec(memory_space=pltpu.HBM)] * 3,
+        out_specs=(vmem, vmem, vmem),
         scratch_shapes=[
             pltpu.VMEM((experts * tokens, features + META), bf16),
             pltpu.VMEM((experts, capacity, hidden_units), bf16),
@@ -363,18 +359,14 @@
             pltpu.VMEM((2, half, slots // 2), bf16),
             pltpu.VMEM((2, half, slots // 2), bf16),
             pltpu.VMEM((half, features), f32),
-            pltpu.VMEM((experts, capacity, hidden_units), bf16),
-            pltpu.VMEM((half, features), bf16),
             pltpu.VMEM((experts, 8, 128), f32),
             pltpu.VMEM((experts, 8, 128), f32),
             dma,
             dma((16,)),
             dma,
-            dma((16,)),
-            dma((features // TILE,)),
-            dma((16,)),
-            dma((16,)),
-            dma((5,)),
+            dma((16, 2)),
+            dma((16, 2)),
+            dma((5, 2)),
             dma,
             dma,
             dma((2,)),
@@ -383,7 +375,7 @@
             dma((16,)),
         ],
         compiler_params=pltpu.CompilerParams(
-            collective_id=0, has_side_effects=True, vmem_limit_bytes=58 * 1024 * 1024
+            collective_id=0, has_side_effects=True, vmem_limit_bytes=48 * 1024 * 1024
         ),
         cost_estimate=pl.CostEstimate(
             flops=4 * slots * hidden_units * features,

time: 44.2 us -> 42.4 us (0.959)
  Pallas kernels: 37.3 us -> 35.1 us
    pallas_call x1, Pallas kernels: 37.3 us -> 35.1 us  [on_pair(): pl.pallas_call(fused_kernel, out_shape=(jax.ShapeDtypeStruct((experts, ca...]
    unnamed x5 -> x11, local copies, waits for them, and re-layouts: 5.98 us -> 6.38 us
where the time goes in v3:
time: 42.4 us; the launch traced here: 42.2 us
  Pallas kernels  35.1 us (83%)
  local copies, waits for them, and re-layouts  6.38 us (15%)
  between operations  0.65 us (2%)
    pallas_call x1, Pallas kernels, on_pair(): pl.pallas_call(fused_kernel, out_shape=(jax.ShapeDtypeStruct((experts, ca...  35.1 us
    unnamed x11, local copies, waits for them, and re-layouts  6.38 us

profile of v3, /device:TPU:0, one launch (start us, length us, event | category | flops | bytes accessed | tf_op | source)
XLA Modules:
  0.0 42.2 jit_solution(15611063925184494180)
XLA Ops:
  0.6 0.0 copy-start
  0.6 1.2 %copy-done = bf16[1,1,16,24,1280]{4,3,2,1,0:T(8,128)(2,1)S(1)} copy-done((bf16[1,1,16,24,1280]{4,3,2,1,0:T(8,128)(2,1)S(1)}, bf16[1,1,16,24,1280]{4,3,2,1,0:T(8,128)(2,1)}, u32[]{:S(2)}) %copy-start) | copy-done | bytes 983064
  1.8 0.0 copy-start.1
  1.8 0.9 %copy-done.1 = bf16[32,1792]{1,0:T(8,128)(2,1)S(1)} copy-done((bf16[32,1792]{1,0:T(8,128)(2,1)S(1)}, bf16[32,1792]{1,0:T(8,128)(2,1)}, u32[]{:S(2)}) %copy-start.1) | copy-done | bytes 114712
  2.7 0.0 copy-start.2
  2.7 0.7 %copy-done.2 = s32[32,8]{0,1:T(8,128)S(1)} copy-done((s32[32,8]{0,1:T(8,128)S(1)}, s32[32,8]{0,1:T(8,128)}, u32[]{:S(2)}) %copy-start.2) | copy-done | bytes 1048
  3.4 0.0 copy-start.3
  3.4 0.7 %copy-done.3 = bf16[32,8]{0,1:T(8,128)(2,1)S(1)} copy-done((bf16[32,8]{0,1:T(8,128)(2,1)S(1)}, bf16[32,8]{0,1:T(8,128)(2,1)}, u32[]{:S(2)}) %copy-start.3) | copy-done | bytes 536
  4.1 35.1 %shard_map.76 = (bf16[16,24,1280]{2,1,0:T(8,128)(2,1)S(1)}, bf16[640,1792]{1,0:T(8,128)(2,1)S(1)}, f32[8,32]{1,0:T(8,128)S(1)}) custom-call(s32[8,32]{1,0:T(8,128)S(1)} %bitcast.11, bf16[8,32]{1,0:T(8,128)(2,1)S(1)} %bitcast.12, bf16[32,1792]{1,0:T(8,128)(2,1)S(1)} %copy-done.1, bf16[16,24,1280]{2,1,0:T(8,128)(2,1)S(1)} %bitcast.10, bf16[1280,1792]{1,0:T(8,128)(2,1)} %bitcast.13), custom_call_target="tpu_custom_call" | custom-call | flops 3523215360 | bytes 10000000 | tf_op jit(solution)/shard_map/pallas_call | solution.py:343
  39.2 0.9 %copy.11 = bf16[1,1,16,24,1280]{4,3,2,1,0:T(8,128)(2,1)} copy(bf16[1,1,16,24,1280]{4,3,2,1,0:T(8,128)(2,1)S(1)} %bitcast.8) | data formatting | bytes 1966080
  40.2 1.4 %copy.12 = bf16[1,640,1792]{2,1,0:T(8,128)(2,1)} copy(bf16[1,640,1792]{2,1,0:T(8,128)(2,1)S(1)} %bitcast.7) | data formatting | bytes 4587520
  41.6 0.6 %copy.13 = f32[32,8]{0,1:T(8,128)} copy(f32[32,8]{0,1:T(8,128)S(1)} %bitcast.9) | data formatting | bytes 2048
Async XLA Ops:
  0.6 1.2 %copy-start = (bf16[1,1,16,24,1280]{4,3,2,1,0:T(8,128)(2,1)S(1)}, bf16[1,1,16,24,1280]{4,3,2,1,0:T(8,128)(2,1)}, u32[]{:S(2)}) copy-start(bf16[1,1,16,24,1280]{4,3,2,1,0:T(8,128)(2,1)} %param.8) | copy-start | bytes 2949124
  1.8 0.9 %copy-start.1 = (bf16[32,1792]{1,0:T(8,128)(2,1)S(1)}, bf16[32,1792]{1,0:T(8,128)(2,1)}, u32[]{:S(2)}) copy-start(bf16[32,1792]{1,0:T(8,128)(2,1)} %go_hbm.1) | copy-start | bytes 344068
  2.7 0.7 %copy-start.2 = (s32[32,8]{0,1:T(8,128)S(1)}, s32[32,8]{0,1:T(8,128)}, u32[]{:S(2)}) copy-start(s32[32,8]{0,1:T(8,128)} %param.6) | copy-start | bytes 3076
  3.4 0.7 %copy-start.3 = (bf16[32,8]{0,1:T(8,128)(2,1)S(1)}, bf16[32,8]{0,1:T(8,128)(2,1)}, u32[]{:S(2)}) copy-start(bf16[32,8]{0,1:T(8,128)(2,1)} %param.7) | copy-start | bytes 1540
